TPU v7x, 512 devices: a whole 4x8x8 slice. The times are simulated.
512 devices in a mesh: ctx: 32 (over x, z), head: 16 (over y, core).
Axes of the slice: x: 4, y: 8, z: 8, core: 2. Of those that a mesh axis runs over, the one named last changes fastest.
Arguments:
- query: bfloat16 [8192, 6144], P('ctx', 'head'), may hold values from -6 to 6
- keys: bfloat16 [8192, 6144], P('ctx', 'head'), may hold values from -6 to 6
- values: bfloat16 [8192, 6144], P('ctx', 'head'), may hold values from -6 to 6
- span_slot: int32 [128], replicated, may hold values from 0 to 127, each once
- span_doc: int32 [128], replicated, may hold values from 0 to 3, never falling along the last dimension, each value on 1 to 64 neighbouring positions
- w_out: bfloat16 [6144, 6144], P('head', 'ctx'), may hold values from -0.078125 to 0.078125
Outputs:
- mixed: bfloat16 [8192, 6144], P(('ctx', 'head'))
Inputs may be any that keep to these rules, and one draw needn't show every extreme that they name: `span_slot`: a permutation of the spans of the clip. `span_doc`: never falls along the clip; one sequence holds exactly 64 spans.
All inputs are finite; a program needn't handle non-finite values.
Results may differ from a plain program's by a relative error of at most 0.024.
Values may be sent and summed in bfloat16 or wider, within the bound.
A program may use at most 64 MiB of HBM per device.

v0:
```python
import jax
import jax.numpy as jnp
from jax import lax
from jax.sharding import PartitionSpec as P

HEAD_DIM = 128
SPAN = 64


def attend_block(carry, q_heads, visible_all, k_rows, v_rows, start):
    top, total, accum = carry
    count = k_rows.shape[0]
    heads = q_heads.shape[1]
    visible = lax.dynamic_slice_in_dim(visible_all, start, count, 1)
    k_heads = k_rows.reshape(count, heads, HEAD_DIM)
    v_heads = v_rows.reshape(count, heads, HEAD_DIM)
    scores = jnp.einsum(
        "qhd,khd->hqk", q_heads, k_heads, preferred_element_type=jnp.float32
    ) * HEAD_DIM ** (-0.5)
    masked = jnp.where(visible[None], scores, jnp.float32(-1e30))
    new_top = jnp.maximum(top, jnp.max(masked, axis=2))
    shrink = jnp.exp(top - new_top)
    weights = jnp.where(visible[None], jnp.exp(scores - new_top[:, :, None]), jnp.float32(0.0))
    total = total * shrink + jnp.sum(weights, axis=2)
    accum = accum * shrink[:, :, None] + jnp.einsum(
        "hqk,khd->hqd", weights.astype(jnp.bfloat16), v_heads, preferred_element_type=jnp.float32
    )
    return (new_top, total, accum)


def attend_piece(carry, q_heads, visible_all, k_rows, v_rows):
    count = k_rows.shape[0]
    width_keys = 1024
    steps = count // width_keys
    k_split = k_rows.reshape(steps, width_keys, k_rows.shape[1])
    v_split = v_rows.reshape(steps, width_keys, v_rows.shape[1])

    def advance(state, items):
        k_part, v_part, offset = items
        return (attend_block(state, q_heads, visible_all, k_part, v_part, offset), None)

    offsets = jnp.arange(steps, dtype=jnp.int32) * width_keys
    carry, unused = lax.scan(advance, carry, (k_split, v_split, offsets))
    return carry


def local(query, keys, values, span_slot, span_doc, w_out):
    rows = query.shape[0]
    width = query.shape[1]
    heads = width // HEAD_DIM
    me_ctx = lax.axis_index("ctx")
    token_span = jnp.repeat(span_slot, SPAN)
    token_doc = jnp.repeat(span_doc[span_slot], SPAN)
    q_span = lax.dynamic_slice_in_dim(token_span, me_ctx * rows, rows, 0)
    q_doc = lax.dynamic_slice_in_dim(token_doc, me_ctx * rows, rows, 0)
    visible_all = (q_doc[:, None] == token_doc[None, :]) & (token_span[None, :] <= q_span[:, None])
    q_heads = query.reshape(rows, heads, HEAD_DIM)
    init = (
        jnp.full((heads, rows), -1e30, jnp.float32),
        jnp.zeros((heads, rows), jnp.float32),
        jnp.zeros((heads, rows, HEAD_DIM), jnp.float32),
    )
    top, total, accum = attend_piece(
        init,
        q_heads,
        visible_all,
        lax.all_gather(keys, "ctx", axis=0, tiled=True),
        lax.all_gather(values, "ctx", axis=0, tiled=True),
    )
    attn = (accum / total[:, :, None]).transpose(1, 0, 2).reshape(rows, width).astype(jnp.bfloat16)
    partial_terms = jnp.dot(
        attn, lax.all_gather(w_out, "ctx", axis=1, tiled=True), preferred_element_type=jnp.float32
    )
    return lax.psum_scatter(
        partial_terms.astype(jnp.bfloat16), "head", scatter_dimension=0, tiled=True
    )


def solution(mesh):
    placed = (P("ctx", "head"), P("ctx", "head"), P("ctx", "head"), P(), P(), P("head", "ctx"))
    return jax.shard_map(
        local, mesh=mesh, in_specs=placed, out_specs=P(("ctx", "head"), None), check_vma=False
    )
```

profile of v0, /device:TPU:6, one launch (start us, length us, event | category | flops | bytes accessed | tf_op | source)
XLA Modules:
  0.0 402.4 jit_solution(11456014154008133694)
XLA Ops:
  13.7 6.2 %compare_and_fusion = pred[256,8192]{0,1:T(8,128)(4,1)} fusion(s32[256]{0:T(256)S(1)} %dynamic_slice.21, s32[256]{0:T(256)S(1)} %dynamic_slice.20, s32[8192]{0:T(1024)S(1)} %le.15, s32[8192]{0:T(1024)S(1)} %reshape.31), kind=kLoop, calls=%fused_computation.24 | loop fusion | flops 6291456 | bytes 2164736 | tf_op jit(solution)/shard_map/and | solution.py:56
  19.9 88.1 %all-gather.4.cloned.1.call-done = bf16[8192,384]{1,0:T(8,128)(2,1)} async-done(((bf16[256,384]{1,0:T(8,128)(2,1)}), bf16[8192,384]{1,0:T(8,128)(2,1)}) %all-gather.4.cloned.1.call-update) | async-done | bytes 6291472 | tf_op jit(solution)/shard_map/all_gather | solution.py:67
  108.0 94.5 %all-gather.6.cloned.1.call-done = bf16[8192,384]{1,0:T(8,128)(2,1)} async-done(((bf16[256,384]{1,0:T(8,128)(2,1)}), bf16[8192,384]{1,0:T(8,128)(2,1)}) %all-gather.6.cloned.1.call-update) | async-done | bytes 6291472 | tf_op jit(solution)/shard_map/all_gather | solution.py:68
  202.5 124.4 %while.15 = (s32[]{:T(128)}, f32[3,256]{1,0:T(4,128)S(1)}, f32[3,256]{1,0:T(4,128)S(1)}, f32[3,256,128]{2,1,0:T(8,128)}, s32[8]{0:T(128)S(1)}, /*index=5*/pred[2...) while((s32[]{:T(128)}, f32[3,256]{1,0:T(4,128)S(1)}, ...), condition=%wide.region_3.4_spmd.clone, body=%wide.region_0.3_spmd.clone.sunk | while | flops 411602688 | bytes 19644600 | solution.py:43
  206.3 2.4 constant_dynamic-slice_fusion.6
  212.6 2.3 copy.30
  214.9 3.0 fusion.37
  221.8 2.4 constant_dynamic-slice_fusion.6
  225.4 1.9 fusion.34
  228.1 2.3 copy.30
  230.4 3.1 fusion.37
  237.3 2.4 constant_dynamic-slice_fusion.6
  243.6 2.3 copy.30
  245.9 3.1 fusion.37
  252.9 2.4 constant_dynamic-slice_fusion.6
  259.2 2.4 copy.30
  261.6 3.1 fusion.37
  268.5 2.4 constant_dynamic-slice_fusion.6
  272.2 1.9 fusion.34
  274.9 2.3 copy.30
  277.2 3.1 fusion.37
  284.1 2.4 constant_dynamic-slice_fusion.6
  290.4 2.3 copy.30
  292.7 3.1 fusion.37
  299.7 2.4 constant_dynamic-slice_fusion.6
  306.0 2.3 copy.30
  308.3 3.1 fusion.37
  315.2 2.4 constant_dynamic-slice_fusion.6
  321.5 2.3 copy.30
  323.8 3.1 fusion.37
  328.2 5.8 %convolution_convert_fusion = bf16[256,6144]{1,0:T(8,128)(2,1)} fusion(bf16[256,384]{0,1:T(8,128)(2,1)S(1)} %bitcast.53, bf16[384,6144]{0,1:T(8,128)(2,1)} %all-gather.8.cloned.1.call-done), kind=kOutput, calls=%fused_computation.25 | convolution fusion | flops 1209532416 | bytes 8060928 | tf_op jit(solution)/shard_map/dot_general | solution.py:71
  334.1 61.8 %reduce-scatter.2.cloned.1.call-done = bf16[16,6144]{1,0:T(8,128)(2,1)} async-done(((bf16[256,6144]{1,0:T(8,128)(2,1)}), bf16[16,6144]{1,0:T(8,128)(2,1)}) %reduce-scatter.2.cloned.1.call-update) | async-done | bytes 196624 | tf_op jit(solution)/shard_map/reduce_scatter | solution.py:74
  (90 shorter events, 49.5 us)
Async XLA Ops:
  6.5 3.0 copy-start
  6.5 101.5 %all-gather.4.cloned.1.call-start = ((), (), s32[]{:S(2)}) async-start(), calls=%async_computation.1 | async-start | bytes 6488064 | tf_op jit(solution)/shard_map/all_gather | solution.py:67
  7.3 195.3 %all-gather.6.cloned.1.call-start = ((), (), s32[]{:S(2)}) async-start(), calls=%async_computation.2 | async-start | bytes 6488064 | tf_op jit(solution)/shard_map/all_gather | solution.py:68
  8.0 320.2 %all-gather.8.cloned.1.call-start = ((), (), s32[]{:S(2)}) async-start(), calls=%async_computation.3 | async-start | bytes 4866048 | tf_op jit(solution)/shard_map/all_gather | solution.py:72
  8.7 387.2 %reduce-scatter.2.cloned.1.call-start = ((), (), s32[]{:S(2)}) async-start(), calls=%async_computation.4 | async-start | bytes 3342336 | tf_op jit(solution)/shard_map/reduce_scatter | solution.py:74
Sparse Core Ops, SparseCore 0:
  10.5 97.4 all-gather.3
  111.2 91.2 all-gather.5
  205.7 86.6 all-gather.7
  334.2 61.6 reduce-scatter.1
where the time goes:
time: 404 us; the launch traced here: 402 us
  waiting for transfers between devices  247 us (61%)
  local copies, waits for them, and re-layouts  67.2 us (17%)
  matrix products  46.4 us (11%)
  loops' own time  16.3 us (4%)
  between operations  13.2 us (3%)
  other arithmetic  12.7 us (3%)
    all_gather x1, waiting for transfers between devices, local(): lax.all_gather(values, 'ctx', axis=0, tiled=True)  94.5 us
    all_gather x1, waiting for transfers between devices, local(): lax.all_gather(keys, 'ctx', axis=0, tiled=True)  88.1 us
    reduce_scatter x1, waiting for transfers between devices, local(): lax.psum_scatter(partial_terms.astype(jnp.bfloat16), 'head', scatter_dime...  61.8 us
    dynamic_slice x32, local copies, waits for them, and re-layouts, attend_piece(): carry, unused = lax.scan(advance, carry, (k_split, v_split, offsets))  52.7 us
    dot_general x8, matrix products, attend_block(): jnp.einsum('hqk,khd->hqd', weights.astype(jnp.bfloat16), v_heads, preferr...  25 us
    another operation x1, loops' own time, attend_piece(): carry, unused = lax.scan(advance, carry, (k_split, v_split, offsets))  16.3 us
    dot_general x8, matrix products, attend_block(): jnp.einsum('qhd,khd->hqk', q_heads, k_heads, preferred_element_type=jnp.f...  15.5 us
    dynamic_slice x8, local copies, waits for them, and re-layouts, attend_block(): visible = lax.dynamic_slice_in_dim(visible_all, start, count, 1)  9.07 us
  transfers between devices with their start and end apart: 4, of which 3 were waited for; matrix products, arithmetic and copies ran while one was open for 30% of the time, Pallas kernels for 0%

commit v1 on v0

v1 whole, which is shorter than its diff:
```python
import math

import jax
import jax.numpy as jnp
from jax import lax
from jax.experimental import pallas as pl
from jax.experimental.pallas import tpu as pltpu
from jax.sharding import PartitionSpec as P

HEAD_DIM = 128
SPAN = 64
NX, NZ, NY = 4, 8, 8
ROWS = 256
HELD = 3
BLOCK = NX * ROWS
WCOLS = 192
WROWS = HELD * HEAD_DIM
PIECE = NZ * WCOLS
D = NX * PIECE
MINE = 16
MASKED = -1e30
SCALE = math.log2(math.e) / math.sqrt(HEAD_DIM)
MESH = pl.DeviceIdType.MESH
RIGHT, LEFT = 0, 1
NT = (((1,), (1,)), ((), ()))


def wrap(value, size):
    return lax.rem(value + 2 * size, size)


def kernel(
    q_hbm, k_hbm, v_hbm, w_hbm, slot_ref, doc_ref, out_ref,
    qb, hot, kb, vb, seen, bias, wb, top, acc, ost, ob,
    prod, sib_out, sib_in, rs_out, rs_in,
    own_sem, s1_send, s1_recv, kv_send, kv_recv, wz_send, wz_recv,
    wx_send, wx_recv, wy_send, wy_recv, o_send, o_recv,
    sib_send, sib_recv, rs_send, rs_recv,
):
    ctx, head = lax.axis_index("ctx"), lax.axis_index("head")
    x, z = lax.div(ctx, NZ), lax.rem(ctx, NZ)
    y, core = lax.div(head, 2), lax.rem(head, 2)

    def at_x(to):
        return (to * NZ + z, head)

    def at_z(to):
        return (x * NZ + to, head)

    def at_y(to):
        return (ctx, to * 2 + core)

    sibling = (ctx, y * 2 + 1 - core)
    z_side = (wrap(z + 1, NZ), wrap(z - 1, NZ))
    x_side = (wrap(x + 1, NX), wrap(x - 1, NX))
    y_side = (wrap(y + 1, NY), wrap(y - 1, NY))

    def remote(src, dst, send, recv, device):
        return pltpu.make_async_remote_copy(
            src_ref=src, dst_ref=dst, send_sem=send, recv_sem=recv,
            device_id=device, device_id_type=MESH,
        )

    def head_of(ring):
        return lax.div(ring + 1, 2)

    def columns(ring):
        return pl.ds(pl.multiple_of(head_of(ring) * HEAD_DIM, HEAD_DIM), HEAD_DIM)

    own = [
        pltpu.make_async_copy(w_hbm, wb.at[x, z], own_sem.at[0]),
        pltpu.make_async_copy(k_hbm.at[:, columns(x)], kb.at[z, x], own_sem.at[1]),
        pltpu.make_async_copy(v_hbm.at[:, columns(x)], vb.at[z, x], own_sem.at[2]),
        pltpu.make_async_copy(q_hbm.at[:, columns(x)], qb.at[x], own_sem.at[3]),
    ]
    for copy in own:
        copy.start()

    barrier = pltpu.get_barrier_semaphore()
    peers = [at_x(wrap(x + step, NX)) for step in (1, 2, 3)]
    peers += [at_z(z_side[0]), at_z(z_side[1]), at_y(y_side[0]), at_y(y_side[1]), sibling]
    for peer in peers:
        pl.semaphore_signal(barrier, inc=1, device_id=peer, device_id_type=MESH)
    pl.semaphore_wait(barrier, len(peers))

    def first(kind, step):
        to = wrap(x + step, NX)
        src = (k_hbm, v_hbm, q_hbm)[kind].at[:, columns(to)]
        dst = qb.at[x] if kind == 2 else (kb, vb)[kind].at[z, x]
        return remote(src, dst, s1_send.at[kind, step - 1], s1_recv.at[kind, step - 1], at_x(to))

    def first_arrived(kind, step):
        by = wrap(x - step, NX)
        dst = qb.at[by] if kind == 2 else (kb, vb)[kind].at[z, by]
        remote(dst, dst, s1_send.at[kind, step - 1], s1_recv.at[kind, step - 1], at_x(by)).wait_recv()

    def ring_piece(buf, owner, side, step, whole, cut):
        if step < NZ // 2 - 1:
            return whole(buf, owner)
        return cut(buf, owner, side)

    def w_whole(buf, owner):
        return buf.at[owner]

    def w_cut(buf, owner, side):
        return buf.at[owner, pl.ds(side * (WCOLS // 2), WCOLS // 2)]

    def kv_whole(buf, owner):
        return buf.at[owner]

    def kv_cut(buf, owner, side):
        return buf.at[owner, pl.ds(side * (NX // 2), NX // 2)]

    def toward(side, step):
        return wrap(z - step, NZ) if side == RIGHT else wrap(z + step, NZ)

    def wz(side, step):
        piece = ring_piece(wb.at[x], toward(side, step), side, step, w_whole, w_cut)
        return remote(piece, piece, wz_send.at[side, step], wz_recv.at[side, step], at_z(z_side[side]))

    def wz_arrived(side, step):
        piece = ring_piece(wb.at[x], toward(side, step + 1), side, step, w_whole, w_cut)
        remote(piece, piece, wz_send.at[side, step], wz_recv.at[side, step], at_z(z_side[side])).wait_recv()

    def kv(kind, side, step):
        piece = ring_piece((kb, vb)[kind], toward(side, step), side, step, kv_whole, kv_cut)
        return remote(
            piece, piece, kv_send.at[kind, side, step], kv_recv.at[kind, side, step], at_z(z_side[side])
        )

    def kv_arrived(kind, side, step):
        piece = ring_piece((kb, vb)[kind], toward(side, step + 1), side, step, kv_whole, kv_cut)
        remote(
            piece, piece, kv_send.at[kind, side, step], kv_recv.at[kind, side, step], at_z(z_side[side])
        ).wait_recv()

    order = [z]
    for step in range(1, NZ // 2):
        order += [wrap(z - step, NZ), wrap(z + step, NZ)]
    order += [wrap(z + NZ // 2, NZ)]

    def wx(side, at):
        piece = wb.at[x, order[at]]
        return remote(piece, piece, wx_send.at[side, at], wx_recv.at[side, at], at_x(x_side[side]))

    def wx_arrived(side, at):
        piece = wb.at[x_side[1 - side], order[at]]
        remote(piece, piece, wx_send.at[side, at], wx_recv.at[side, at], at_x(x_side[side])).wait_recv()

    def wy(side, at):
        piece = wb.at[x_side[1 - side], order[at], pl.ds(side * (WCOLS // 2), WCOLS // 2)]
        return remote(piece, piece, wy_send.at[side, at], wy_recv.at[side, at], at_x(x_side[side]))

    def wy_arrived(side, at):
        piece = wb.at[wrap(x + 2, NX), order[at], pl.ds(side * (WCOLS // 2), WCOLS // 2)]
        remote(piece, piece, wy_send.at[side, at], wy_recv.at[side, at], at_x(x_side[side])).wait_recv()

    def spread(at):
        for side in (RIGHT, LEFT):
            wx(side, at).start()

    def hand_on(at):
        for side in (RIGHT, LEFT):
            wx_arrived(side, at)
            wy(side, at).start()

    for kind in (0, 1):
        for step in (1, 2, 3):
            first(kind, step).start()
    own[0].wait()
    for side in (RIGHT, LEFT):
        wz(side, 0).start()
    for step in (1, 2, 3):
        first(2, step).start()
    spread(0)

    rows_at = lax.broadcasted_iota(jnp.int32, (128, 128), 0)
    lanes_at = lax.broadcasted_iota(jnp.int32, (128, 128), 1)
    zero = jnp.zeros((128, 128), jnp.float32)
    slot_row = jnp.broadcast_to(slot_ref[...].astype(jnp.float32), (128, 128))
    doc_row = jnp.broadcast_to(doc_ref[...].astype(jnp.float32), (128, 128))
    clip = jnp.sum(jnp.where(rows_at == lanes_at, slot_row, zero), axis=1, keepdims=True)
    clip = jnp.broadcast_to(clip, (128, 128))
    doc = jnp.sum(jnp.where(clip == lanes_at.astype(jnp.float32), doc_row, zero), axis=1, keepdims=True)
    doc = jnp.broadcast_to(doc, (128, 128))
    start = jnp.sum(jnp.where(doc_row < doc, zero + 1.0, zero), axis=1, keepdims=True)
    start = jnp.broadcast_to(start, (128, 128))
    spans = ROWS // SPAN
    wanted = (lax.div(lanes_at, spans) * NZ + z) * spans + lax.rem(lanes_at, spans)
    chosen = rows_at == wanted
    clip_q = jnp.sum(jnp.where(chosen, clip, zero), axis=0, keepdims=True)
    start_q = jnp.sum(jnp.where(chosen, start, zero), axis=0, keepdims=True)
    visible = (clip <= clip_q) & (clip >= start_q)
    seen[...] = jnp.where(visible, zero, zero + MASKED)

    def expand(zz, unused):
        for at in range(NX * spans):
            slot = (at // spans * NZ + zz) * spans + at % spans
            row = jnp.broadcast_to(seen[pl.ds(slot, 1), :], (SPAN, 128))
            bias[zz, pl.ds(at * SPAN, SPAN), :] = row.astype(jnp.bfloat16)
        return unused

    lax.fori_loop(0, NZ, expand, 0)
    span_at = lax.div(lax.broadcasted_iota(jnp.int32, (ROWS, 128), 0), SPAN)
    lane_at = lax.broadcasted_iota(jnp.int32, (ROWS, 128), 1)
    for part in range(NX):
        hot[part] = jnp.where(lane_at == span_at + part * spans, 1.0, 0.0).astype(jnp.bfloat16)
    top[...] = jnp.full(top.shape, MASKED, jnp.float32)
    acc[...] = jnp.zeros(acc.shape, jnp.float32)

    def tile(block, part):
        q_all = jnp.concatenate([qb[part], hot[part]], axis=1)
        k_all = jnp.concatenate([kb[block].reshape(BLOCK, HEAD_DIM), bias[block]], axis=1)
        v_all = vb[block].reshape(BLOCK, HEAD_DIM)
        v_all = jnp.concatenate([v_all, jnp.ones((BLOCK, 128), jnp.bfloat16)], axis=1)
        scores = lax.dot_general(q_all, k_all, NT, preferred_element_type=jnp.float32)
        old = top[part]
        new = jnp.maximum(old, jnp.broadcast_to(jnp.max(scores, axis=1, keepdims=True), old.shape))
        scaled = new * SCALE
        weights = jnp.exp2(scores * SCALE - jnp.concatenate([scaled] * (BLOCK // 128), axis=1))
        shrink = jnp.exp2(old * SCALE - scaled)
        fresh = jnp.dot(weights.astype(jnp.bfloat16), v_all, preferred_element_type=jnp.float32)
        acc[part] = acc[part] * jnp.concatenate([shrink, shrink], axis=1) + fresh
        top[part] = new

    def attend_two(one, other):
        def body(at, unused):
            tile(jnp.where(at < NX, one, other), lax.rem(at, NX))
            return unused
        lax.fori_loop(0, 2 * NX, body, 0)

    def w_step(step):
        for side in (RIGHT, LEFT):
            wz_arrived(side, step)
            wz(side, step + 1).start()
        spread(2 * step + 1)
        spread(2 * step + 2)

    w_step(0)
    for kind in (0, 1):
        for step in (1, 2, 3):
            first_arrived(kind, step)
        own[1 + kind].wait()
        for side in (RIGHT, LEFT):
            kv(kind, side, 0).start()
    w_step(1)
    for step in (1, 2, 3):
        first_arrived(2, step)
    own[3].wait()

    def attend_own(part, unused):
        tile(z, part)
        return unused

    lax.fori_loop(0, NX, attend_own, 0)
    w_step(2)
    for side in (RIGHT, LEFT):
        wz_arrived(side, 3)
    spread(7)

    for step in (0, 1, 2):
        for kind in (0, 1):
            for side in (RIGHT, LEFT):
                kv_arrived(kind, side, step)
                kv(kind, side, step + 1).start()
        attend_two(wrap(z - step - 1, NZ), wrap(z + step + 1, NZ))
        if step < 2:
            for at in range(4 * step, 4 * step + 4):
                hand_on(at)
    for kind in (0, 1):
        for side in (RIGHT, LEFT):
            kv_arrived(kind, side, 3)

    mine = head_of(x)

    def gives(part):
        half = (x == 1) & (part < 2) | (x == 2) & (part >= 2)
        return (x == 0) | (x == 3) | half

    def answer(part):
        return remote(ost.at[part], ob.at[mine], o_send.at[part], o_recv.at[mine], at_x(part))

    def attend_last(part, unused):
        tile(wrap(z + NZ // 2, NZ), part)
        result = acc[part]
        result = (result[:, :HEAD_DIM] / result[:, HEAD_DIM:]).astype(jnp.bfloat16)
        ost[part] = result

        @pl.when(gives(part) & (part != x))
        def _():
            answer(part).start()

        @pl.when(gives(part) & (part == x))
        def _():
            ob[mine] = result

        return unused

    lax.fori_loop(0, NX, attend_last, 0)
    for side in (RIGHT, LEFT):
        for at in range(NZ):
            wy_arrived(side, at)
    for index in range(HELD):
        giver = jnp.where(x < 2, 1, 2) if index == 1 else (0, 0, 3)[index]

        @pl.when(giver != x)
        def _():
            remote(
                ost.at[0], ob.at[index], o_send.at[0], o_recv.at[index], at_x(wrap(x + 1, NX))
            ).wait_recv()

    attn = jnp.concatenate([ob[0], ob[1], ob[2]], axis=1)

    def to_sibling(piece):
        return remote(sib_out.at[piece], sib_in.at[piece], sib_send.at[piece], sib_recv.at[piece], sibling)

    for piece in range(NX):
        part = lax.dot_general(
            attn, wb[piece].reshape(PIECE, WROWS), NT, preferred_element_type=jnp.float32
        )
        prod[piece] = part.reshape(NY, 2, MINE, PIECE)
        sib_out[piece] = prod[piece, :, 1 - core].astype(jnp.bfloat16)
        to_sibling(piece).start()

    def rs(side, step, piece):
        return remote(
            rs_out.at[side, step, piece], rs_in.at[side, step, piece],
            rs_send.at[side, step, piece], rs_recv.at[side, step, piece], at_y(y_side[side]),
        )

    def here(piece, owner):
        return prod[piece, owner, core] + sib_in[piece, owner].astype(jnp.float32)

    def travels(side, step, piece):
        return step > 0 or piece // (NX // 2) == side

    for step in range(NY // 2):
        for piece in range(NX):
            if step == 0:
                to_sibling(piece).wait_recv()
            for side in (RIGHT, LEFT):
                if not travels(side, step, piece):
                    continue
                away = NY // 2 - step
                total = here(piece, wrap(y + away if side == RIGHT else y - away, NY))
                if step > 0 and travels(side, step - 1, piece):
                    rs(side, step - 1, piece).wait_recv()
                    total = total + rs_in[side, step - 1, piece].astype(jnp.float32)
                rs_out[side, step, piece] = total.astype(jnp.bfloat16)
                rs(side, step, piece).start()
    for piece in range(NX):
        total = here(piece, y)
        for side in (RIGHT, LEFT):
            rs(side, NY // 2 - 1, piece).wait_recv()
            total = total + rs_in[side, NY // 2 - 1, piece].astype(jnp.float32)
        out_ref[:, pl.ds(piece * PIECE, PIECE)] = total.astype(jnp.bfloat16)

    for kind in (0, 1, 2):
        for step in (1, 2, 3):
            first(kind, step).wait_send()
    for side in (RIGHT, LEFT):
        for step in range(NZ // 2):
            wz(side, step).wait_send()
            for kind in (0, 1):
                kv(kind, side, step).wait_send()
        for at in range(NZ):
            wx(side, at).wait_send()
            wy(side, at).wait_send()
    for part in range(NX):
        @pl.when(gives(part) & (part != x))
        def _():
            answer(part).wait_send()
    for piece in range(NX):
        to_sibling(piece).wait_send()
    for step in range(NY // 2):
        for piece in range(NX):
            for side in (RIGHT, LEFT):
                if travels(side, step, piece):
                    rs(side, step, piece).wait_send()


def local(query, keys, values, span_slot, span_doc, w_out):
    whole = pl.BlockSpec(memory_space=pltpu.VMEM)
    remote = pl.BlockSpec(memory_space=pl.ANY)
    bf16, f32 = jnp.bfloat16, jnp.float32
    dma = pltpu.SemaphoreType.DMA
    return pl.pallas_call(
        kernel,
        out_shape=jax.ShapeDtypeStruct((MINE, D), bf16),
        in_specs=[remote] * 4 + [whole] * 2,
        out_specs=whole,
        scratch_shapes=[
            pltpu.VMEM((NX, ROWS, HEAD_DIM), bf16),
            pltpu.VMEM((NX, ROWS, 128), bf16),
            pltpu.VMEM((NZ, NX, ROWS, HEAD_DIM), bf16),
            pltpu.VMEM((NZ, NX, ROWS, HEAD_DIM), bf16),
            pltpu.VMEM((128, 128), f32),
            pltpu.VMEM((NZ, BLOCK, 128), bf16),
            pltpu.VMEM((NX, NZ, WCOLS, WROWS), bf16),
            pltpu.VMEM((NX, ROWS, 128), f32),
            pltpu.VMEM((NX, ROWS, 256), f32),
            pltpu.VMEM((NX, ROWS, HEAD_DIM), bf16),
            pltpu.VMEM((HELD, ROWS, HEAD_DIM), bf16),
            pltpu.VMEM((NX, NY, 2, MINE, PIECE), f32),
            pltpu.VMEM((NX, NY, MINE, PIECE), bf16),
            pltpu.VMEM((NX, NY, MINE, PIECE), bf16),
            pltpu.VMEM((2, NY // 2, NX, MINE, PIECE), bf16),
            pltpu.VMEM((2, NY // 2, NX, MINE, PIECE), bf16),
            dma((4,)),
            dma((3, 3)), dma((3, 3)),
            dma((2, 2, NZ // 2)), dma((2, 2, NZ // 2)),
            dma((2, NZ // 2)), dma((2, NZ // 2)),
            dma((2, NZ)), dma((2, NZ)),
            dma((2, NZ)), dma((2, NZ)),
            dma((NX,)), dma((HELD,)),
            dma((NX,)), dma((NX,)),
            dma((2, NY // 2, NX)), dma((2, NY // 2, NX)),
        ],
        compiler_params=pltpu.CompilerParams(
            collective_id=0, has_side_effects=True, vmem_limit_bytes=56 << 20
        ),
        cost_estimate=pl.CostEstimate(
            flops=2 * BLOCK * 8192 * 512 + 2 * ROWS * WROWS * D,
            bytes_accessed=1 << 21, transcendentals=BLOCK * 8192,
        ),
    )(query, keys, values, w_out.T, span_slot.reshape(1, 128), span_doc.reshape(1, 128))


def solution(mesh):
    placed = (P("ctx", "head"), P("ctx", "head"), P("ctx", "head"), P(), P(), P("head", "ctx"))
    return jax.shard_map(
        local, mesh=mesh, in_specs=placed, out_specs=P(("ctx", "head"), None), check_vma=False
    )
```

time: 404 us -> 106 us (0.26)
  waiting for transfers between devices: 247 us -> 0 us
  Pallas kernels: 0 us -> 104 us
  local copies, waits for them, and re-layouts: 67.2 us -> 1.62 us
  matrix products: 46.4 us -> 0 us
  loops' own time: 16.3 us -> 0 us
  between operations: 13.2 us -> 0.01 us
  other arithmetic: 12.7 us -> 0 us
    all_gather x3 -> x0, waiting for transfers between devices: 183 us -> none  [the longest x1 94.5 us: local(): lax.all_gather(values, 'ctx', axis=0, tiled=True)]
    pallas_call x0 -> x1, Pallas kernels: none -> 104 us  [local(): pl.pallas_call(kernel, out_shape=jax.ShapeDtypeStruct((MINE, D), bf16), i...]
    dynamic_slice x42 -> x0, local copies, waits for them, and re-layouts: 61.9 us -> none  [the longest x32 52.7 us: attend_piece(): carry, unused = lax.scan(advance, carry, (k_split, v_split, offsets))]
    reduce_scatter x1 -> x0, waiting for transfers between devices: 61.8 us -> none  [local(): lax.psum_scatter(partial_terms.astype(jnp.bfloat16), 'head', scatter_dime...]
    dot_general x17 -> x0, matrix products: 46.4 us -> none  [the longest x8 25 us: attend_block(): jnp.einsum('hqk,khd->hqd', weights.astype(jnp.bfloat16), v_heads, preferr...]
    another operation x1 -> x0, loops' own time: 16.3 us -> none  [attend_piece(): carry, unused = lax.scan(advance, carry, (k_split, v_split, offsets))]
    and x1 -> x0, other arithmetic: 6.2 us -> none  [local(): (q_doc[:, None] == token_doc[None, :]) & (token_span[None, :] <= q_span[:...]
    reduce_sum x8 -> x0, other arithmetic: 5.58 us -> none  [attend_block(): total = total * shrink + jnp.sum(weights, axis=2)]
  transfers between devices with their start and end apart: 4 -> 0, of which waited for: 3 -> 0; matrix products, arithmetic and copies ran while one was open for 30% -> 0% of each run, Pallas kernels for 0% -> 0%
where the time goes in v1:
time: 106 us; the launch traced here: 105 us
  Pallas kernels  104 us (98%)
  local copies, waits for them, and re-layouts  1.62 us (2%)
    pallas_call x1, Pallas kernels, local(): pl.pallas_call(kernel, out_shape=jax.ShapeDtypeStruct((MINE, D), bf16), i...  104 us

profile of v1, /device:TPU:6, one launch (start us, length us, event | category | flops | bytes accessed | tf_op | source)
XLA Modules:
  0.0 105.4 jit_solution(3593164105208228463)
XLA Ops:
  0.0 103.8 %shard_map.64 = bf16[16,6144]{1,0:T(8,128)(2,1)} custom-call(bf16[256,384]{1,0:T(8,128)(2,1)} %q_hbm.1, bf16[256,384]{1,0:T(8,128)(2,1)} %k_hbm.1, bf16[256,384]{1,0:T(8,128)(2,1)} %v_hbm.1, bf16[192,384]{1,0:T(8,128)(2,1)} %bitcast.3, s32[1,128]{1,0:T(1,128)} %bitcast.4, s32[1,128]{1,0:T(1,128)} %bitcast.5), custom_call_target="tpu_custom_call" | custom-call | flops 9797894144 | bytes 2097152 | tf_op jit(solution)/shard_map/pallas_call | solution.py:387
  103.8 1.6 %copy.8 = bf16[16,6144]{1,0:T(8,128)(2,1)} copy(bf16[16,6144]{1,0:T(8,128)(2,1)} %shard_map.64) | data formatting | bytes 393216

commit v2 on v1

v2 whole, which is shorter than its diff:
```python
import math

import jax
import jax.numpy as jnp
from jax import lax
from jax.experimental import pallas as pl
from jax.experimental.pallas import tpu as pltpu
from jax.sharding import PartitionSpec as P

HEAD_DIM = 128
SPAN = 64
NX, NZ, NY = 4, 8, 8
ROWS = 256
HELD = 3
BLOCK = NX * ROWS
WCOLS = 192
WROWS = HELD * HEAD_DIM
PIECE = NZ * WCOLS
D = NX * PIECE
MINE = 16
MASKED = -1e30
LOWEST = -2e30
CUT = 96
SCALE = math.log2(math.e) / math.sqrt(HEAD_DIM)
MESH = pl.DeviceIdType.MESH
RIGHT, LEFT = 0, 1
NT = (((1,), (1,)), ((), ()))


def wrap(value, size):
    return lax.rem(value + 2 * size, size)


def kernel(
    q_hbm, k_hbm, v_hbm, w_hbm, slot_ref, doc_ref, out_ref,
    qb, hot, kb, vb, seen, bias, wb, top, acc, ost, ob, stat_out, stat_in,
    prod, sib_out, sib_in, rs_out, rs_in,
    own_sem, s1_send, s1_recv, kv0_send, kv0_recv, kv_send, kv_recv, wz_send, wz_recv,
    wx_send, wx_recv, wy_send, wy_recv, o_send, o_recv, stat_send, stat_recv,
    sib_send, sib_recv, rs_send, rs_recv,
):
    ctx, head = lax.axis_index("ctx"), lax.axis_index("head")
    x, z = lax.div(ctx, NZ), lax.rem(ctx, NZ)
    y, core = lax.div(head, 2), lax.rem(head, 2)

    def at_x(to):
        return (to * NZ + z, head)

    def at_z(to):
        return (x * NZ + to, head)

    def at_y(to):
        return (ctx, to * 2 + core)

    sibling = (ctx, y * 2 + 1 - core)
    z_side = (wrap(z + 1, NZ), wrap(z - 1, NZ))
    x_side = (wrap(x + 1, NX), wrap(x - 1, NX))
    y_side = (wrap(y + 1, NY), wrap(y - 1, NY))

    def remote(src, dst, send, recv, device):
        return pltpu.make_async_remote_copy(
            src_ref=src, dst_ref=dst, send_sem=send, recv_sem=recv,
            device_id=device, device_id_type=MESH,
        )

    def is_full(ring):
        edge = jnp.where((ring == 0) | (ring == NX - 1), 1, 0)
        return edge + core == 1

    def head_of(ring):
        return jnp.where(is_full(ring), 2 * lax.div(ring, 2), 1)

    def columns(ring):
        return pl.ds(pl.multiple_of(head_of(ring) * HEAD_DIM, HEAD_DIM), HEAD_DIM)

    def place(ring, source):
        return jnp.where(is_full(ring), source, lax.rem(source, 2))

    def wants(ring, source):
        return is_full(ring) | (lax.div(ring, 2) == lax.div(source, 2))

    full = is_full(x)
    not_full = jnp.logical_not(full)
    halves = jnp.where(full, 2, 1)

    own = [
        pltpu.make_async_copy(w_hbm, wb.at[x, z], own_sem.at[0]),
        pltpu.make_async_copy(k_hbm.at[:, columns(x)], kb.at[z, place(x, x)], own_sem.at[1]),
        pltpu.make_async_copy(v_hbm.at[:, columns(x)], vb.at[z, place(x, x)], own_sem.at[2]),
        pltpu.make_async_copy(q_hbm.at[:, columns(x)], qb.at[x], own_sem.at[3]),
    ]
    for copy in own:
        copy.start()

    barrier = pltpu.get_barrier_semaphore()
    peers = [at_x(wrap(x + step, NX)) for step in (1, 2, 3)]
    peers += [at_z(z_side[0]), at_z(z_side[1]), at_y(y_side[0]), at_y(y_side[1]), sibling]
    for peer in peers:
        pl.semaphore_signal(barrier, inc=1, device_id=peer, device_id_type=MESH)
    pl.semaphore_wait(barrier, len(peers))

    def first(kind, step):
        to = wrap(x + step, NX)
        src = (k_hbm, v_hbm, q_hbm)[kind].at[:, columns(to)]
        dst = qb.at[x] if kind == 2 else (kb, vb)[kind].at[z, place(to, x)]
        return remote(src, dst, s1_send.at[kind, step - 1], s1_recv.at[kind, step - 1], at_x(to))

    def first_arrived(kind, step):
        by = wrap(x - step, NX)
        dst = qb.at[by] if kind == 2 else (kb, vb)[kind].at[z, place(x, by)]
        remote(dst, dst, s1_send.at[kind, step - 1], s1_recv.at[kind, step - 1], at_x(by)).wait_recv()

    def toward(side, step):
        return wrap(z - step, NZ) if side == RIGHT else wrap(z + step, NZ)

    def wz_piece(side, owner, step):
        if step < NZ // 2 - 1:
            return wb.at[x, owner]
        return wb.at[x, owner, pl.ds(side * (WCOLS // 2), WCOLS // 2)]

    def wz(side, step):
        piece = wz_piece(side, toward(side, step), step)
        return remote(piece, piece, wz_send.at[side, step], wz_recv.at[side, step], at_z(z_side[side]))

    def wz_arrived(side, step):
        piece = wz_piece(side, toward(side, step + 1), step)
        remote(piece, piece, wz_send.at[side, step], wz_recv.at[side, step], at_z(z_side[side])).wait_recv()

    def kv0(kind, side, at, owner):
        piece = (kb, vb)[kind].at[owner, at]
        return remote(
            piece, piece, kv0_send.at[kind, side, at], kv0_recv.at[kind, side, at], at_z(z_side[side])
        )

    def kv(kind, side, step, half, owner):
        piece = (kb, vb)[kind].at[owner, pl.ds(2 * half, 2)]
        return remote(
            piece, piece, kv_send.at[kind, side, step - 1, half], kv_recv.at[kind, side, step - 1, half],
            at_z(z_side[side]),
        )

    def kv3(kind, side, owner, count):
        piece = (kb, vb)[kind].at[owner, pl.ds(side * count, count)]
        return remote(
            piece, piece, kv_send.at[kind, side, 2, 0], kv_recv.at[kind, side, 2, 0], at_z(z_side[side])
        )

    order = [z]
    for step in range(1, NZ // 2):
        order += [wrap(z - step, NZ), wrap(z + step, NZ)]
    order += [wrap(z + NZ // 2, NZ)]

    def wx(side, at):
        piece = wb.at[x, order[at]]
        return remote(piece, piece, wx_send.at[side, at], wx_recv.at[side, at], at_x(x_side[side]))

    def wx_arrived(side, at):
        piece = wb.at[x_side[1 - side], order[at]]
        remote(piece, piece, wx_send.at[side, at], wx_recv.at[side, at], at_x(x_side[side])).wait_recv()

    def wy_rows(side):
        return pl.ds(0, CUT) if side == RIGHT else pl.ds(CUT, WCOLS - CUT)

    def wy(side, at):
        piece = wb.at[x_side[1 - side], order[at], wy_rows(side)]
        return remote(piece, piece, wy_send.at[side, at], wy_recv.at[side, at], at_x(x_side[side]))

    def wy_arrived(side, at):
        piece = wb.at[wrap(x + 2, NX), order[at], wy_rows(side)]
        remote(piece, piece, wy_send.at[side, at], wy_recv.at[side, at], at_x(x_side[side])).wait_recv()

    def spread(at):
        for side in (RIGHT, LEFT):
            wx(side, at).start()

    def hand_on(at):
        for side in (RIGHT, LEFT):
            wx_arrived(side, at)
            wy(side, at).start()

    for kind in (0, 1):
        for step in (1, 3, 2):
            @pl.when(wants(wrap(x + step, NX), x))
            def _():
                first(kind, step).start()
    own[0].wait()
    for side in (RIGHT, LEFT):
        wz(side, 0).start()
    for kind in (0, 1):
        own[1 + kind].wait()
        for side in (RIGHT, LEFT):
            kv0(kind, side, place(x, x), z).start()
    for step in (1, 3, 2):
        first(2, step).start()
    spread(0)

    rows_at = lax.broadcasted_iota(jnp.int32, (128, 128), 0)
    lanes_at = lax.broadcasted_iota(jnp.int32, (128, 128), 1)
    zero = jnp.zeros((128, 128), jnp.float32)
    slot_row = jnp.broadcast_to(slot_ref[...].astype(jnp.float32), (128, 128))
    doc_row = jnp.broadcast_to(doc_ref[...].astype(jnp.float32), (128, 128))
    clip = jnp.sum(jnp.where(rows_at == lanes_at, slot_row, zero), axis=1, keepdims=True)
    clip = jnp.broadcast_to(clip, (128, 128))
    doc = jnp.sum(jnp.where(clip == lanes_at.astype(jnp.float32), doc_row, zero), axis=1, keepdims=True)
    doc = jnp.broadcast_to(doc, (128, 128))
    start = jnp.sum(jnp.where(doc_row < doc, zero + 1.0, zero), axis=1, keepdims=True)
    start = jnp.broadcast_to(start, (128, 128))
    spans = ROWS // SPAN
    wanted = (lax.div(lanes_at, spans) * NZ + z) * spans + lax.rem(lanes_at, spans)
    chosen = rows_at == wanted
    clip_q = jnp.sum(jnp.where(chosen, clip, zero), axis=0, keepdims=True)
    start_q = jnp.sum(jnp.where(chosen, start, zero), axis=0, keepdims=True)
    visible = (clip <= clip_q) & (clip >= start_q)
    seen[...] = jnp.where(visible, zero, zero + MASKED)

    def expand(zz, unused):
        for at in range(NX):
            source = jnp.where(full, at, lax.rem(2 * lax.div(x, 2) + at, NX))
            for span in range(spans):
                row = seen[pl.ds((source * NZ + zz) * spans + span, 1), :]
                row = jnp.broadcast_to(row, (SPAN, 128)).astype(jnp.bfloat16)
                bias[zz, at, pl.ds(span * SPAN, SPAN), :] = row
        return unused

    lax.fori_loop(0, NZ, expand, 0)
    span_at = lax.div(lax.broadcasted_iota(jnp.int32, (ROWS, 128), 0), SPAN)
    lane_at = lax.broadcasted_iota(jnp.int32, (ROWS, 128), 1)
    for part in range(NX):
        hot[part] = jnp.where(lane_at == span_at + part * spans, 1.0, 0.0).astype(jnp.bfloat16)
    top[...] = jnp.full(top.shape, LOWEST, jnp.float32)
    acc[...] = jnp.zeros(acc.shape, jnp.float32)

    def attend(block, half, tiles, parts):
        count = tiles * ROWS
        held = pl.ds(2 * half, tiles)
        k_all = jnp.concatenate(
            [kb[block, held].reshape(count, HEAD_DIM), bias[block, held].reshape(count, 128)], axis=1
        )
        v_all = jnp.concatenate(
            [vb[block, held].reshape(count, HEAD_DIM), jnp.ones((count, 128), jnp.bfloat16)], axis=1
        )
        for part in parts:
            q_all = jnp.concatenate([qb[part], hot[part]], axis=1)
            scores = lax.dot_general(q_all, k_all, NT, preferred_element_type=jnp.float32)
            old = top[part]
            new = jnp.maximum(old, jnp.broadcast_to(jnp.max(scores, axis=1, keepdims=True), old.shape))
            scaled = new * SCALE
            weights = jnp.exp2(scores * SCALE - jnp.concatenate([scaled] * (count // 128), axis=1))
            shrink = jnp.exp2(old * SCALE - scaled)
            fresh = jnp.dot(weights.astype(jnp.bfloat16), v_all, preferred_element_type=jnp.float32)
            acc[part] = acc[part] * jnp.concatenate([shrink, shrink], axis=1) + fresh
            top[part] = new

    def w_step(step):
        for side in (RIGHT, LEFT):
            wz_arrived(side, step)
            wz(side, step + 1).start()
        spread(2 * step + 1)
        spread(2 * step + 2)

    w_step(0)
    for step in (1, 3, 2):
        by = wrap(x - step, NX)

        @pl.when(wants(x, by))
        def _():
            for kind in (0, 1):
                first_arrived(kind, step)
                for side in (RIGHT, LEFT):
                    kv0(kind, side, place(x, by), z).start()
    w_step(1)
    for step in (1, 2, 3):
        first_arrived(2, step)
    own[3].wait()

    def attend_own(half, unused):
        attend(z, half, 2, range(NX))
        return unused

    lax.fori_loop(0, halves, attend_own, 0)
    w_step(2)
    for side in (RIGHT, LEFT):
        wz_arrived(side, 3)
    spread(7)

    for step in (0, 1, 2):
        def half_step(half, unused):
            for kind in (0, 1):
                for side in (RIGHT, LEFT):
                    owner = toward(side, step + 1)
                    if step == 0:
                        for at in (0, 1):
                            kv0(kind, side, 2 * half + at, owner).wait_recv()
                    else:
                        kv(kind, side, step, half, owner).wait_recv()
                    if step < 2:
                        kv(kind, side, step + 1, half, owner).start()
                    else:
                        @pl.when(full & (half == side))
                        def _():
                            kv3(kind, side, owner, 2).start()

                        @pl.when(not_full)
                        def _():
                            kv3(kind, side, owner, 1).start()

            def body(at, unused):
                attend(jnp.where(at == 0, toward(RIGHT, step + 1), toward(LEFT, step + 1)), half, 2, range(NX))
                return unused

            lax.fori_loop(0, 2, body, 0)
            return unused

        lax.fori_loop(0, halves, half_step, 0)
        if step < 2:
            for at in range(4 * step, 4 * step + 4):
                hand_on(at)

    def answer(part):
        return remote(ost.at[part], ob.at[x], o_send.at[part], o_recv.at[x], at_x(part))

    def answer_stat(part):
        return remote(
            stat_out.at[part], stat_in.at[x], stat_send.at[part], stat_recv.at[x], at_x(part)
        )

    eye = rows_at == lanes_at

    def finish(part):
        total = acc[part]
        result = (total[:, :HEAD_DIM] / total[:, HEAD_DIM:]).astype(jnp.bfloat16)
        ost[part] = result

        @pl.when(part != x)
        def _():
            answer(part).start()

        @pl.when(part == x)
        def _():
            ob[x] = result

        @pl.when(not_full)
        def _():
            scaled = top[part] * SCALE
            sums = total[:, HEAD_DIM:]
            rows = []
            for which in (scaled, sums):
                for at in (0, 128):
                    rows.append(jnp.sum(jnp.where(eye, which[at:at + 128], zero), axis=0, keepdims=True))
            stats = jnp.concatenate(rows + [zero[:4]], axis=0)
            stat_out[part] = stats

            @pl.when(part != x)
            def _():
                answer_stat(part).start()

            @pl.when(part == x)
            def _():
                stat_in[x] = stats

    last = wrap(z + NZ // 2, NZ)

    def arrive_last(count):
        for kind in (0, 1):
            for side in (RIGHT, LEFT):
                kv3(kind, side, last, count).wait_recv()

    def end_with(tiles):
        def body(pair, unused):
            parts = (2 * pair, 2 * pair + 1)
            attend(last, 0, tiles, parts)
            for part in parts:
                finish(part)
            return unused
        lax.fori_loop(0, 2, body, 0)

    @pl.when(full)
    def _():
        arrive_last(2)
        end_with(4)

    @pl.when(not_full)
    def _():
        arrive_last(1)
        end_with(2)

    for giver in range(NX):
        @pl.when(giver != x)
        def _():
            remote(ost.at[0], ob.at[giver], o_send.at[0], o_recv.at[giver], at_x(x_side[0])).wait_recv()

            @pl.when(jnp.logical_not(is_full(giver)))
            def _():
                remote(
                    stat_out.at[0], stat_in.at[giver], stat_send.at[0], stat_recv.at[giver], at_x(x_side[0])
                ).wait_recv()

    def column(stats, first_row):
        parts = []
        for at in (first_row, first_row + 1):
            row = jnp.broadcast_to(stats[at:at + 1], (128, 128))
            whole = jnp.sum(jnp.where(eye, row, zero), axis=1, keepdims=True)
            parts.append(jnp.broadcast_to(whole, (128, 128)))
        return jnp.concatenate(parts, axis=0)

    one, two = 1 - core, 2 + core
    top_one, top_two = column(stat_in[one], 0), column(stat_in[two], 0)
    best = jnp.maximum(top_one, top_two)
    share_one = column(stat_in[one], 2) * jnp.exp2(top_one - best)
    share_two = column(stat_in[two], 2) * jnp.exp2(top_two - best)
    middle = ob[one].astype(jnp.float32) * share_one + ob[two].astype(jnp.float32) * share_two
    middle = (middle / (share_one + share_two)).astype(jnp.bfloat16)
    attn = jnp.concatenate([ob[core], middle, ob[NX - 1 - core]], axis=1)

    def to_sibling(piece):
        return remote(sib_out.at[piece], sib_in.at[piece], sib_send.at[piece], sib_recv.at[piece], sibling)

    def rs(side, step, piece):
        return remote(
            rs_out.at[side, step, piece], rs_in.at[side, step, piece],
            rs_send.at[side, step, piece], rs_recv.at[side, step, piece], at_y(y_side[side]),
        )

    def here(piece, owner):
        return prod[piece, owner, core] + sib_in[piece, owner].astype(jnp.float32)

    def travels(side, step, piece):
        return step > 0 or piece // (NX // 2) == side

    def pass_on(side, step, piece):
        away = NY // 2 - step
        total = here(piece, wrap(y + away if side == RIGHT else y - away, NY))
        if step > 0 and travels(side, step - 1, piece):
            rs(side, step - 1, piece).wait_recv()
            total = total + rs_in[side, step - 1, piece].astype(jnp.float32)
        rs_out[side, step, piece] = total.astype(jnp.bfloat16)
        rs(side, step, piece).start()

    def begin(piece):
        to_sibling(piece).wait_recv()
        side = piece // (NX // 2)
        pass_on(side, 0, piece)
        pass_on(1 - side, 1, piece)

    for side in (RIGHT, LEFT):
        for at in range(NZ):
            wy_arrived(side, at)
    turn = (0, 2, 1, 3)
    for index, piece in enumerate(turn):
        part = lax.dot_general(
            attn, wb[piece].reshape(PIECE, WROWS), NT, preferred_element_type=jnp.float32
        )
        prod[piece] = part.reshape(NY, 2, MINE, PIECE)
        sib_out[piece] = prod[piece, :, 1 - core].astype(jnp.bfloat16)
        to_sibling(piece).start()
        if index:
            begin(turn[index - 1])
    begin(turn[-1])
    late = ((2, 3, 0, 1), (0, 1, 2, 3))
    for at in (0, 1):
        for side in (RIGHT, LEFT):
            pass_on(side, 1, late[side][2 + at])
    for step in range(2, NY // 2):
        for at in range(NX):
            for side in (RIGHT, LEFT):
                pass_on(side, step, late[side][at])
    for piece in (2, 0, 3, 1):
        total = here(piece, y)
        for side in (RIGHT, LEFT):
            rs(side, NY // 2 - 1, piece).wait_recv()
            total = total + rs_in[side, NY // 2 - 1, piece].astype(jnp.float32)
        out_ref[:, pl.ds(piece * PIECE, PIECE)] = total.astype(jnp.bfloat16)

    for step in (1, 2, 3):
        first(2, step).wait_send()

        @pl.when(wants(wrap(x + step, NX), x))
        def _():
            for kind in (0, 1):
                first(kind, step).wait_send()

    def sent(half, unused):
        for kind in (0, 1):
            for side in (RIGHT, LEFT):
                for at in (0, 1):
                    kv0(kind, side, 2 * half + at, z).wait_send()
                for step in (1, 2):
                    kv(kind, side, step, half, z).wait_send()
        return unused

    lax.fori_loop(0, halves, sent, 0)
    for kind in (0, 1):
        for side in (RIGHT, LEFT):
            @pl.when(full)
            def _():
                kv3(kind, side, z, 2).wait_send()

            @pl.when(not_full)
            def _():
                kv3(kind, side, z, 1).wait_send()
    for side in (RIGHT, LEFT):
        for step in range(NZ // 2):
            wz(side, step).wait_send()
        for at in range(NZ):
            wx(side, at).wait_send()
            wy(side, at).wait_send()
    for part in range(NX):
        @pl.when(part != x)
        def _():
            answer(part).wait_send()

            @pl.when(not_full)
            def _():
                answer_stat(part).wait_send()
    for piece in range(NX):
        to_sibling(piece).wait_send()
    for step in range(NY // 2):
        for piece in range(NX):
            for side in (RIGHT, LEFT):
                if travels(side, step, piece):
                    rs(side, step, piece).wait_send()


def local(query, keys, values, span_slot, span_doc, w_out):
    whole = pl.BlockSpec(memory_space=pltpu.VMEM)
    remote = pl.BlockSpec(memory_space=pl.ANY)
    bf16, f32 = jnp.bfloat16, jnp.float32
    dma = pltpu.SemaphoreType.DMA
    return pl.pallas_call(
        kernel,
        out_shape=jax.ShapeDtypeStruct((MINE, D), bf16),
        in_specs=[remote] * 4 + [whole] * 2,
        out_specs=whole,
        scratch_shapes=[
            pltpu.VMEM((NX, ROWS, HEAD_DIM), bf16),
            pltpu.VMEM((NX, ROWS, 128), bf16),
            pltpu.VMEM((NZ, NX, ROWS, HEAD_DIM), bf16),
            pltpu.VMEM((NZ, NX, ROWS, HEAD_DIM), bf16),
            pltpu.VMEM((128, 128), f32),
            pltpu.VMEM((NZ, NX, ROWS, 128), bf16),
            pltpu.VMEM((NX, NZ, WCOLS, WROWS), bf16),
            pltpu.VMEM((NX, ROWS, 128), f32),
            pltpu.VMEM((NX, ROWS, 256), f32),
            pltpu.VMEM((NX, ROWS, HEAD_DIM), bf16),
            pltpu.VMEM((NX, ROWS, HEAD_DIM), bf16),
            pltpu.VMEM((NX, 8, 128), f32),
            pltpu.VMEM((NX, 8, 128), f32),
            pltpu.VMEM((NX, NY, 2, MINE, PIECE), f32),
            pltpu.VMEM((NX, NY, MINE, PIECE), bf16),
            pltpu.VMEM((NX, NY, MINE, PIECE), bf16),
            pltpu.VMEM((2, NY // 2, NX, MINE, PIECE), bf16),
            pltpu.VMEM((2, NY // 2, NX, MINE, PIECE), bf16),
            dma((4,)),
            dma((3, 3)), dma((3, 3)),
            dma((2, 2, NX)), dma((2, 2, NX)),
            dma((2, 2, 3, 2)), dma((2, 2, 3, 2)),
            dma((2, NZ // 2)), dma((2, NZ // 2)),
            dma((2, NZ)), dma((2, NZ)),
            dma((2, NZ)), dma((2, NZ)),
            dma((NX,)), dma((NX,)),
            dma((NX,)), dma((NX,)),
            dma((NX,)), dma((NX,)),
            dma((2, NY // 2, NX)), dma((2, NY // 2, NX)),
        ],
        compiler_params=pltpu.CompilerParams(
            collective_id=0, has_side_effects=True, vmem_limit_bytes=56 << 20
        ),
        cost_estimate=pl.CostEstimate(
            flops=2 * BLOCK * 8192 * 512 + 2 * ROWS * WROWS * D,
            bytes_accessed=1 << 21, transcendentals=BLOCK * 8192,
        ),
    )(query, keys, values, w_out.T, span_slot.reshape(1, 128), span_doc.reshape(1, 128))


def solution(mesh):
    placed = (P("ctx", "head"), P("ctx", "head"), P("ctx", "head"), P(), P(), P("head", "ctx"))
    return jax.shard_map(
        local, mesh=mesh, in_specs=placed, out_specs=P(("ctx", "head"), None), check_vma=False
    )
```

time: 106 us -> 91.6 us (0.86)
  Pallas kernels: 104 us -> 89.4 us
    pallas_call x1, Pallas kernels: 104 us -> 89.4 us  [local(): pl.pallas_call(kernel, out_shape=jax.ShapeDtypeStruct((MINE, D), bf16), i...]
where the time goes in v2:
time: 91.6 us; the launch traced here: 91 us
  Pallas kernels  89.4 us (98%)
  local copies, waits for them, and re-layouts  1.62 us (2%)
    pallas_call x1, Pallas kernels, local(): pl.pallas_call(kernel, out_shape=jax.ShapeDtypeStruct((MINE, D), bf16), i...  89.4 us

profile of v2, /device:TPU:6, one launch (start us, length us, event | category | flops | bytes accessed | tf_op | source)
XLA Modules:
  0.0 91.0 jit_solution(16749315486037193995)
XLA Ops:
  0.0 89.4 %shard_map.64 = bf16[16,6144]{1,0:T(8,128)(2,1)} custom-call(bf16[256,384]{1,0:T(8,128)(2,1)} %q_hbm.1, bf16[256,384]{1,0:T(8,128)(2,1)} %k_hbm.1, bf16[256,384]{1,0:T(8,128)(2,1)} %v_hbm.1, bf16[192,384]{1,0:T(8,128)(2,1)} %bitcast.3, s32[1,128]{1,0:T(1,128)} %bitcast.4, s32[1,128]{1,0:T(1,128)} %bitcast.5), custom_call_target="tpu_custom_call" | custom-call | flops 9797894144 | bytes 2097152 | tf_op jit(solution)/shard_map/pallas_call | solution.py:529
  89.4 1.6 %copy.8 = bf16[16,6144]{1,0:T(8,128)(2,1)} copy(bf16[16,6144]{1,0:T(8,128)(2,1)} %shard_map.64) | data formatting | bytes 393216

commit v3 on v2

--- a/solution.py
+++ b/solution.py
@@ -35,7 +35,7 @@
     q_hbm, k_hbm, v_hbm, w_hbm, slot_ref, doc_ref, out_ref,
     qb, hot, kb, vb, seen, bias, wb, top, acc, ost, ob, stat_out, stat_in,
     prod, sib_out, sib_in, rs_out, rs_in,
-    own_sem, s1_send, s1_recv, kv0_send, kv0_recv, kv_send, kv_recv, wz_send, wz_recv,
+    own_sem, s1_send, s1_recv, kv_send, kv_recv, wz_send, wz_recv,
     wx_send, wx_recv, wy_send, wy_recv, o_send, o_recv, stat_send, stat_recv,
     sib_send, sib_recv, rs_send, rs_recv,
 ):
@@ -73,8 +73,8 @@
     def columns(ring):
         return pl.ds(pl.multiple_of(head_of(ring) * HEAD_DIM, HEAD_DIM), HEAD_DIM)
 
-    def place(ring, source):
-        return jnp.where(is_full(ring), source, lax.rem(source, 2))
+    def place(ring, step):
+        return jnp.where(is_full(ring), (1, 3, 2)[step - 1], 1)
 
     def wants(ring, source):
         return is_full(ring) | (lax.div(ring, 2) == lax.div(source, 2))
@@ -82,11 +82,12 @@
     full = is_full(x)
     not_full = jnp.logical_not(full)
     halves = jnp.where(full, 2, 1)
+    lead = jnp.where(full, 1, 0)
 
     own = [
         pltpu.make_async_copy(w_hbm, wb.at[x, z], own_sem.at[0]),
-        pltpu.make_async_copy(k_hbm.at[:, columns(x)], kb.at[z, place(x, x)], own_sem.at[1]),
-        pltpu.make_async_copy(v_hbm.at[:, columns(x)], vb.at[z, place(x, x)], own_sem.at[2]),
+        pltpu.make_async_copy(k_hbm.at[:, columns(x)], kb.at[z, 0], own_sem.at[1]),
+        pltpu.make_async_copy(v_hbm.at[:, columns(x)], vb.at[z, 0], own_sem.at[2]),
         pltpu.make_async_copy(q_hbm.at[:, columns(x)], qb.at[x], own_sem.at[3]),
     ]
     for copy in own:
@@ -102,12 +103,12 @@
     def first(kind, step):
         to = wrap(x + step, NX)
         src = (k_hbm, v_hbm, q_hbm)[kind].at[:, columns(to)]
-        dst = qb.at[x] if kind == 2 else (kb, vb)[kind].at[z, place(to, x)]
+        dst = qb.at[x] if kind == 2 else (kb, vb)[kind].at[z, place(to, step)]
         return remote(src, dst, s1_send.at[kind, step - 1], s1_recv.at[kind, step - 1], at_x(to))
 
     def first_arrived(kind, step):
         by = wrap(x - step, NX)
-        dst = qb.at[by] if kind == 2 else (kb, vb)[kind].at[z, place(x, by)]
+        dst = qb.at[by] if kind == 2 else (kb, vb)[kind].at[z, place(x, step)]
         remote(dst, dst, s1_send.at[kind, step - 1], s1_recv.at[kind, step - 1], at_x(by)).wait_recv()
 
     def toward(side, step):
@@ -126,47 +127,46 @@
         piece = wz_piece(side, toward(side, step + 1), step)
         remote(piece, piece, wz_send.at[side, step], wz_recv.at[side, step], at_z(z_side[side])).wait_recv()
 
-    def kv0(kind, side, at, owner):
-        piece = (kb, vb)[kind].at[owner, at]
+    def kv0(kind, side, at):
+        piece, half = (kb, vb)[kind].at[z, at], lax.div(at, 2)
         return remote(
-            piece, piece, kv0_send.at[kind, side, at], kv0_recv.at[kind, side, at], at_z(z_side[side])
+            piece, piece, kv_send.at[kind, side, 0, half], kv_recv.at[kind, side, 0, half], at_z(z_side[side])
         )
 
     def kv(kind, side, step, half, owner):
         piece = (kb, vb)[kind].at[owner, pl.ds(2 * half, 2)]
         return remote(
-            piece, piece, kv_send.at[kind, side, step - 1, half], kv_recv.at[kind, side, step - 1, half],
+            piece, piece, kv_send.at[kind, side, step, half], kv_recv.at[kind, side, step, half],
             at_z(z_side[side]),
         )
 
     def kv3(kind, side, owner, count):
         piece = (kb, vb)[kind].at[owner, pl.ds(side * count, count)]
         return remote(
-            piece, piece, kv_send.at[kind, side, 2, 0], kv_recv.at[kind, side, 2, 0], at_z(z_side[side])
-        )
-
-    order = [z]
-    for step in range(1, NZ // 2):
-        order += [wrap(z - step, NZ), wrap(z + step, NZ)]
-    order += [wrap(z + NZ // 2, NZ)]
+            piece, piece, kv_send.at[kind, side, 3, 0], kv_recv.at[kind, side, 3, 0], at_z(z_side[side])
+        )
+
+    def turn(at):
+        step = lax.div(at + 1, 2)
+        return wrap(jnp.where(lax.rem(at, 2) == 1, z - step, z + step), NZ)
 
     def wx(side, at):
-        piece = wb.at[x, order[at]]
+        piece = wb.at[x, turn(at)]
         return remote(piece, piece, wx_send.at[side, at], wx_recv.at[side, at], at_x(x_side[side]))
 
     def wx_arrived(side, at):
-        piece = wb.at[x_side[1 - side], order[at]]
+        piece = wb.at[x_side[1 - side], turn(at)]
         remote(piece, piece, wx_send.at[side, at], wx_recv.at[side, at], at_x(x_side[side])).wait_recv()
 
     def wy_rows(side):
         return pl.ds(0, CUT) if side == RIGHT else pl.ds(CUT, WCOLS - CUT)
 
     def wy(side, at):
-        piece = wb.at[x_side[1 - side], order[at], wy_rows(side)]
+        piece = wb.at[x_side[1 - side], turn(at), wy_rows(side)]
         return remote(piece, piece, wy_send.at[side, at], wy_recv.at[side, at], at_x(x_side[side]))
 
     def wy_arrived(side, at):
-        piece = wb.at[wrap(x + 2, NX), order[at], wy_rows(side)]
+        piece = wb.at[wrap(x + 2, NX), turn(at), wy_rows(side)]
         remote(piece, piece, wy_send.at[side, at], wy_recv.at[side, at], at_x(x_side[side])).wait_recv()
 
     def spread(at):
@@ -189,10 +189,10 @@
     for kind in (0, 1):
         own[1 + kind].wait()
         for side in (RIGHT, LEFT):
-            kv0(kind, side, place(x, x), z).start()
+            kv0(kind, side, jnp.int32(0)).start()
     for step in (1, 3, 2):
         first(2, step).start()
-    spread(0)
+    spread(jnp.int32(0))
 
     rows_at = lax.broadcasted_iota(jnp.int32, (128, 128), 0)
     lanes_at = lax.broadcasted_iota(jnp.int32, (128, 128), 1)
@@ -215,7 +215,10 @@
 
     def expand(zz, unused):
         for at in range(NX):
-            source = jnp.where(full, at, lax.rem(2 * lax.div(x, 2) + at, NX))
+            partner = 2 * lax.div(x, 2) + 1 - lax.rem(x, 2)
+            source = wrap(x + (0, -1, 1, 2)[at], NX)
+            if at == 1:
+                source = jnp.where(full, source, partner)
             for span in range(spans):
                 row = seen[pl.ds((source * NZ + zz) * spans + span, 1), :]
                 row = jnp.broadcast_to(row, (SPAN, 128)).astype(jnp.bfloat16)
@@ -230,15 +233,18 @@
     top[...] = jnp.full(top.shape, LOWEST, jnp.float32)
     acc[...] = jnp.zeros(acc.shape, jnp.float32)
 
-    def attend(block, half, tiles, parts):
-        count = tiles * ROWS
-        held = pl.ds(2 * half, tiles)
+    def attend(pairs, parts):
+        count = 2 * ROWS
+
+        def join(buf, width):
+            return [buf[block, pl.ds(2 * half, 2)].reshape(count, width) for block, half in pairs]
+
         k_all = jnp.concatenate(
-            [kb[block, held].reshape(count, HEAD_DIM), bias[block, held].reshape(count, 128)], axis=1
-        )
-        v_all = jnp.concatenate(
-            [vb[block, held].reshape(count, HEAD_DIM), jnp.ones((count, 128), jnp.bfloat16)], axis=1
-        )
+            [jnp.concatenate(both, axis=1) for both in zip(join(kb, HEAD_DIM), join(bias, 128))], axis=0
+        )
+        ones = jnp.ones((count, 128), jnp.bfloat16)
+        v_all = jnp.concatenate([jnp.concatenate([v, ones], axis=1) for v in join(vb, HEAD_DIM)], axis=0)
+        count *= len(pairs)
         for part in parts:
             q_all = jnp.concatenate([qb[part], hot[part]], axis=1)
             scores = lax.dot_general(q_all, k_all, NT, preferred_element_type=jnp.float32)
@@ -255,11 +261,10 @@
         for side in (RIGHT, LEFT):
             wz_arrived(side, step)
             wz(side, step + 1).start()
-        spread(2 * step + 1)
-        spread(2 * step + 2)
-
-    w_step(0)
-    for step in (1, 3, 2):
+        spread(jnp.int32(2 * step + 1))
+        spread(jnp.int32(2 * step + 2))
+
+    def tiles_from(step):
         by = wrap(x - step, NX)
 
         @pl.when(wants(x, by))
@@ -267,54 +272,70 @@
             for kind in (0, 1):
                 first_arrived(kind, step)
                 for side in (RIGHT, LEFT):
-                    kv0(kind, side, place(x, by), z).start()
+                    kv0(kind, side, place(x, step)).start()
+
+    w_step(0)
+    tiles_from(1)
+    tiles_from(3)
     w_step(1)
-    for step in (1, 2, 3):
+    tiles_from(2)
+    for step in (1, 3, 2):
         first_arrived(2, step)
     own[3].wait()
 
-    def attend_own(half, unused):
-        attend(z, half, 2, range(NX))
+    per = jnp.where(full, 2, 4)
+
+    def main(index, unused):
+        stage = index - lead
+        step, half = lax.div(stage + halves, halves) - 1, lax.rem(stage + halves, halves)
+        right, left = wrap(z - step - 1, NZ), wrap(z + step + 1, NZ)
+
+        @pl.when(stage >= 0)
+        def _():
+            for kind in (0, 1):
+                for side, owner in ((RIGHT, right), (LEFT, left)):
+                    kv(kind, side, step, half, owner).wait_recv()
+
+                    @pl.when(step < 2)
+                    def _():
+                        kv(kind, side, step + 1, half, owner).start()
+
+                    @pl.when((step == 2) & full & (half == side))
+                    def _():
+                        kv3(kind, side, owner, 2).start()
+
+                    @pl.when((step == 2) & not_full)
+                    def _():
+                        kv3(kind, side, owner, 1).start()
+
+        is_own = stage < 0
+        attend(
+            (
+                (jnp.where(is_own, z, right), jnp.where(is_own, 0, half)),
+                (jnp.where(is_own, z, left), jnp.where(is_own, 1, half)),
+            ),
+            range(NX),
+        )
+
+        @pl.when(stage == 0)
+        def _():
+            w_step(2)
+
+        @pl.when(stage == 1)
+        def _():
+            for side in (RIGHT, LEFT):
+                wz_arrived(side, 3)
+            spread(jnp.int32(7))
+
+        def hand(at, unused):
+            hand_on(at)
+            return unused
+
+        begun = jnp.minimum(per * jnp.maximum(stage - 1, 0), NZ)
+        lax.fori_loop(begun, jnp.minimum(per * jnp.maximum(stage, 0), NZ), hand, 0)
         return unused
 
-    lax.fori_loop(0, halves, attend_own, 0)
-    w_step(2)
-    for side in (RIGHT, LEFT):
-        wz_arrived(side, 3)
-    spread(7)
-
-    for step in (0, 1, 2):
-        def half_step(half, unused):
-            for kind in (0, 1):
-                for side in (RIGHT, LEFT):
-                    owner = toward(side, step + 1)
-                    if step == 0:
-                        for at in (0, 1):
-                            kv0(kind, side, 2 * half + at, owner).wait_recv()
-                    else:
-                        kv(kind, side, step, half, owner).wait_recv()
-                    if step < 2:
-                        kv(kind, side, step + 1, half, owner).start()
-                    else:
-                        @pl.when(full & (half == side))
-                        def _():
-                            kv3(kind, side, owner, 2).start()
-
-                        @pl.when(not_full)
-                        def _():
-                            kv3(kind, side, owner, 1).start()
-
-            def body(at, unused):
-                attend(jnp.where(at == 0, toward(RIGHT, step + 1), toward(LEFT, step + 1)), half, 2, range(NX))
-                return unused
-
-            lax.fori_loop(0, 2, body, 0)
-            return unused
-
-        lax.fori_loop(0, halves, half_step, 0)
-        if step < 2:
-            for at in range(4 * step, 4 * step + 4):
-                hand_on(at)
+    lax.fori_loop(0, lead + 3 * halves, main, 0)
 
     def answer(part):
         return remote(ost.at[part], ob.at[x], o_send.at[part], o_recv.at[x], at_x(part))
@@ -365,24 +386,22 @@
             for side in (RIGHT, LEFT):
                 kv3(kind, side, last, count).wait_recv()
 
-    def end_with(tiles):
-        def body(pair, unused):
-            parts = (2 * pair, 2 * pair + 1)
-            attend(last, 0, tiles, parts)
-            for part in parts:
-                finish(part)
-            return unused
-        lax.fori_loop(0, 2, body, 0)
-
     @pl.when(full)
     def _():
         arrive_last(2)
-        end_with(4)
 
     @pl.when(not_full)
     def _():
         arrive_last(1)
-        end_with(2)
+
+    def end(pair, unused):
+        parts = (2 * pair, 2 * pair + 1)
+        attend(((jnp.where(full, last, z), 0), (last, jnp.where(full, 1, 0))), parts)
+        for part in parts:
+            finish(part)
+        return unused
+
+    lax.fori_loop(0, 2, end, 0)
 
     for giver in range(NX):
         @pl.when(giver != x)
@@ -412,8 +431,16 @@
     middle = (middle / (share_one + share_two)).astype(jnp.bfloat16)
     attn = jnp.concatenate([ob[core], middle, ob[NX - 1 - core]], axis=1)
 
-    def to_sibling(piece):
-        return remote(sib_out.at[piece], sib_in.at[piece], sib_send.at[piece], sib_recv.at[piece], sibling)
+    pieces = (x, x_side[0], x_side[1], wrap(x + 2, NX))
+    owners = [wrap(y + away, NY) for away in (4, 3, -3, 2, -2, 1, -1, 0)]
+    cuts = ((0, 1), (1, 2), (3, 5))
+
+    def to_sibling(piece, cut):
+        rows = pl.ds(*cuts[cut])
+        return remote(
+            sib_out.at[piece, rows], sib_in.at[piece, rows],
+            sib_send.at[piece, cut], sib_recv.at[piece, cut], sibling,
+        )
 
     def rs(side, step, piece):
         return remote(
@@ -421,15 +448,14 @@
             rs_send.at[side, step, piece], rs_recv.at[side, step, piece], at_y(y_side[side]),
         )
 
-    def here(piece, owner):
-        return prod[piece, owner, core] + sib_in[piece, owner].astype(jnp.float32)
+    def here(piece, rank):
+        return prod[piece, owners[rank], core] + sib_in[piece, rank].astype(jnp.float32)
 
     def travels(side, step, piece):
-        return step > 0 or piece // (NX // 2) == side
+        return step > 0 or piece % 2 == side
 
     def pass_on(side, step, piece):
-        away = NY // 2 - step
-        total = here(piece, wrap(y + away if side == RIGHT else y - away, NY))
+        total = here(piece, 2 * step - 1 + side if step else 0)
         if step > 0 and travels(side, step - 1, piece):
             rs(side, step - 1, piece).wait_recv()
             total = total + rs_in[side, step - 1, piece].astype(jnp.float32)
@@ -437,39 +463,45 @@
         rs(side, step, piece).start()
 
     def begin(piece):
-        to_sibling(piece).wait_recv()
-        side = piece // (NX // 2)
-        pass_on(side, 0, piece)
-        pass_on(1 - side, 1, piece)
-
-    for side in (RIGHT, LEFT):
-        for at in range(NZ):
-            wy_arrived(side, at)
-    turn = (0, 2, 1, 3)
-    for index, piece in enumerate(turn):
+        to_sibling(piece, 0).wait_recv()
+        pass_on(piece % 2, 0, piece)
+        to_sibling(piece, 1).wait_recv()
+        pass_on(1 - piece % 2, 1, piece)
+
+    for piece in range(NX):
+        if piece == NX - 1:
+            for side in (RIGHT, LEFT):
+                for at in range(NZ):
+                    wy_arrived(side, jnp.int32(at))
         part = lax.dot_general(
-            attn, wb[piece].reshape(PIECE, WROWS), NT, preferred_element_type=jnp.float32
+            attn, wb[pieces[piece]].reshape(PIECE, WROWS), NT, preferred_element_type=jnp.float32
         )
         prod[piece] = part.reshape(NY, 2, MINE, PIECE)
-        sib_out[piece] = prod[piece, :, 1 - core].astype(jnp.bfloat16)
-        to_sibling(piece).start()
-        if index:
-            begin(turn[index - 1])
-    begin(turn[-1])
-    late = ((2, 3, 0, 1), (0, 1, 2, 3))
-    for at in (0, 1):
+        for rank in range(NY):
+            sib_out[piece, rank] = prod[piece, owners[rank], 1 - core].astype(jnp.bfloat16)
+            if rank in (0, 2):
+                to_sibling(piece, rank // 2).start()
+        if piece:
+            begin(piece - 1)
+    for piece in range(NX):
+        to_sibling(piece, 2).start()
+    begin(NX - 1)
+    late = ((1, 3, 0, 2), (0, 2, 1, 3))
+    for at in (2, 3):
         for side in (RIGHT, LEFT):
-            pass_on(side, 1, late[side][2 + at])
+            pass_on(side, 1, late[side][at])
+    for piece in range(NX):
+        to_sibling(piece, 2).wait_recv()
     for step in range(2, NY // 2):
         for at in range(NX):
             for side in (RIGHT, LEFT):
                 pass_on(side, step, late[side][at])
-    for piece in (2, 0, 3, 1):
-        total = here(piece, y)
+    for piece in (1, 0, 3, 2):
+        total = here(piece, NY - 1)
         for side in (RIGHT, LEFT):
             rs(side, NY // 2 - 1, piece).wait_recv()
             total = total + rs_in[side, NY // 2 - 1, piece].astype(jnp.float32)
-        out_ref[:, pl.ds(piece * PIECE, PIECE)] = total.astype(jnp.bfloat16)
+        out_ref[:, pl.ds(pl.multiple_of(pieces[piece] * PIECE, PIECE), PIECE)] = total.astype(jnp.bfloat16)
 
     for step in (1, 2, 3):
         first(2, step).wait_send()
@@ -482,9 +514,7 @@
     def sent(half, unused):
         for kind in (0, 1):
             for side in (RIGHT, LEFT):
-                for at in (0, 1):
-                    kv0(kind, side, 2 * half + at, z).wait_send()
-                for step in (1, 2):
+                for step in (0, 1, 2):
                     kv(kind, side, step, half, z).wait_send()
         return unused
 
@@ -502,8 +532,8 @@
         for step in range(NZ // 2):
             wz(side, step).wait_send()
         for at in range(NZ):
-            wx(side, at).wait_send()
-            wy(side, at).wait_send()
+            wx(side, jnp.int32(at)).wait_send()
+            wy(side, jnp.int32(at)).wait_send()
     for part in range(NX):
         @pl.when(part != x)
         def _():
@@ -513,7 +543,8 @@
             def _():
                 answer_stat(part).wait_send()
     for piece in range(NX):
-        to_sibling(piece).wait_send()
+        for cut in range(3):
+            to_sibling(piece, cut).wait_send()
     for step in range(NY // 2):
         for piece in range(NX):
             for side in (RIGHT, LEFT):
@@ -552,14 +583,13 @@
             pltpu.VMEM((2, NY // 2, NX, MINE, PIECE), bf16),
             dma((4,)),
             dma((3, 3)), dma((3, 3)),
-            dma((2, 2, NX)), dma((2, 2, NX)),
-            dma((2, 2, 3, 2)), dma((2, 2, 3, 2)),
+            dma((2, 2, 4, 2)), dma((2, 2, 4, 2)),
             dma((2, NZ // 2)), dma((2, NZ // 2)),
             dma((2, NZ)), dma((2, NZ)),
             dma((2, NZ)), dma((2, NZ)),
             dma((NX,)), dma((NX,)),
             dma((NX,)), dma((NX,)),
-            dma((NX,)), dma((NX,)),
+            dma((NX, 3)), dma((NX, 3)),
             dma((2, NY // 2, NX)), dma((2, NY // 2, NX)),
         ],
         compiler_params=pltpu.CompilerParams(

time: 91.6 us -> 88.3 us (0.964)
  Pallas kernels: 89.4 us -> 86.2 us
    pallas_call x1, Pallas kernels: 89.4 us -> 86.2 us  [local(): pl.pallas_call(kernel, out_shape=jax.ShapeDtypeStruct((MINE, D), bf16), i...]
where the time goes in v3:
time: 88.3 us; the launch traced here: 87.8 us
  Pallas kernels  86.2 us (98%)
  local copies, waits for them, and re-layouts  1.62 us (2%)
    pallas_call x1, Pallas kernels, local(): pl.pallas_call(kernel, out_shape=jax.ShapeDtypeStruct((MINE, D), bf16), i...  86.2 us

profile of v3, /device:TPU:6, one launch (start us, length us, event | category | flops | bytes accessed | tf_op | source)
XLA Modules:
  0.0 87.8 jit_solution(1377871150034763767)
XLA Ops:
  0.0 86.2 %shard_map.64 = bf16[16,6144]{1,0:T(8,128)(2,1)} custom-call(bf16[256,384]{1,0:T(8,128)(2,1)} %q_hbm.1, bf16[256,384]{1,0:T(8,128)(2,1)} %k_hbm.1, bf16[256,384]{1,0:T(8,128)(2,1)} %v_hbm.1, bf16[192,384]{1,0:T(8,128)(2,1)} %bitcast.3, s32[1,128]{1,0:T(1,128)} %bitcast.4, s32[1,128]{1,0:T(1,128)} %bitcast.5), custom_call_target="tpu_custom_call" | custom-call | flops 9797894144 | bytes 2097152 | tf_op jit(solution)/shard_map/pallas_call | solution.py:560
  86.2 1.6 %copy.8 = bf16[16,6144]{1,0:T(8,128)(2,1)} copy(bf16[16,6144]{1,0:T(8,128)(2,1)} %shard_map.64) | data formatting | bytes 393216

commit v4 on v3

--- a/solution.py
+++ b/solution.py
@@ -21,6 +21,7 @@
 MASKED = -1e30
 LOWEST = -2e30
 CUT = 96
+EARLY = 4
 SCALE = math.log2(math.e) / math.sqrt(HEAD_DIM)
 MESH = pl.DeviceIdType.MESH
 RIGHT, LEFT = 0, 1
@@ -283,7 +284,7 @@
         first_arrived(2, step)
     own[3].wait()
 
-    per = jnp.where(full, 2, 4)
+    per = jnp.where(full, 1, 2)
 
     def main(index, unused):
         stage = index - lead
@@ -331,8 +332,8 @@
             hand_on(at)
             return unused
 
-        begun = jnp.minimum(per * jnp.maximum(stage - 1, 0), NZ)
-        lax.fori_loop(begun, jnp.minimum(per * jnp.maximum(stage, 0), NZ), hand, 0)
+        begun = jnp.minimum(per * jnp.maximum(stage - 1, 0), EARLY)
+        lax.fori_loop(begun, jnp.minimum(per * jnp.maximum(stage, 0), EARLY), hand, 0)
         return unused
 
     lax.fori_loop(0, lead + 3 * halves, main, 0)
@@ -403,6 +404,10 @@
 
     lax.fori_loop(0, 2, end, 0)
 
+    for at in range(EARLY, NZ):
+        hand_on(jnp.int32(at))
+
+
     for giver in range(NX):
         @pl.when(giver != x)
         def _():
@@ -470,6 +475,7 @@
 
     for piece in range(NX):
         if piece == NX - 1:
+            begin(NX - 2)
             for side in (RIGHT, LEFT):
                 for at in range(NZ):
                     wy_arrived(side, jnp.int32(at))
@@ -481,7 +487,7 @@
             sib_out[piece, rank] = prod[piece, owners[rank], 1 - core].astype(jnp.bfloat16)
             if rank in (0, 2):
                 to_sibling(piece, rank // 2).start()
-        if piece:
+        if piece in (1, 2):
             begin(piece - 1)
     for piece in range(NX):
         to_sibling(piece, 2).start()
@@ -496,13 +502,6 @@
         for at in range(NX):
             for side in (RIGHT, LEFT):
                 pass_on(side, step, late[side][at])
-    for piece in (1, 0, 3, 2):
-        total = here(piece, NY - 1)
-        for side in (RIGHT, LEFT):
-            rs(side, NY // 2 - 1, piece).wait_recv()
-            total = total + rs_in[side, NY // 2 - 1, piece].astype(jnp.float32)
-        out_ref[:, pl.ds(pl.multiple_of(pieces[piece] * PIECE, PIECE), PIECE)] = total.astype(jnp.bfloat16)
-
     for step in (1, 2, 3):
         first(2, step).wait_send()
 
@@ -545,11 +544,21 @@
     for piece in range(NX):
         for cut in range(3):
             to_sibling(piece, cut).wait_send()
-    for step in range(NY // 2):
+    for step in range(NY // 2 - 1):
         for piece in range(NX):
             for side in (RIGHT, LEFT):
                 if travels(side, step, piece):
                     rs(side, step, piece).wait_send()
+
+    for piece in (1, 0, 3, 2):
+        total = here(piece, NY - 1)
+        for side in (RIGHT, LEFT):
+            rs(side, NY // 2 - 1, piece).wait_recv()
+            total = total + rs_in[side, NY // 2 - 1, piece].astype(jnp.float32)
+        out_ref[:, pl.ds(pl.multiple_of(pieces[piece] * PIECE, PIECE), PIECE)] = total.astype(jnp.bfloat16)
+    for piece in range(NX):
+        for side in (RIGHT, LEFT):
+            rs(side, NY // 2 - 1, piece).wait_send()
 
 
 def local(query, keys, values, span_slot, span_doc, w_out):

time: 88.3 us -> 88 us (level)
  no operation moved by 1% of the time
where the time goes in v4:
time: 88 us; the launch traced here: 87.1 us
  Pallas kernels  85.5 us (97%)
  local copies, waits for them, and re-layouts  1.62 us (2%)
    pallas_call x1, Pallas kernels, local(): pl.pallas_call(kernel, out_shape=jax.ShapeDtypeStruct((MINE, D), bf16), i...  85.5 us

profile of v4, /device:TPU:6, one launch (start us, length us, event | category | flops | bytes accessed | tf_op | source)
XLA Modules:
  0.0 87.1 jit_solution(7631347661126723000)
XLA Ops:
  0.0 85.5 %shard_map.64 = bf16[16,6144]{1,0:T(8,128)(2,1)} custom-call(bf16[256,384]{1,0:T(8,128)(2,1)} %q_hbm.1, bf16[256,384]{1,0:T(8,128)(2,1)} %k_hbm.1, bf16[256,384]{1,0:T(8,128)(2,1)} %v_hbm.1, bf16[192,384]{1,0:T(8,128)(2,1)} %bitcast.3, s32[1,128]{1,0:T(1,128)} %bitcast.4, s32[1,128]{1,0:T(1,128)} %bitcast.5), custom_call_target="tpu_custom_call" | custom-call | flops 9797894144 | bytes 2097152 | tf_op jit(solution)/shard_map/pallas_call | solution.py:569
  85.5 1.6 %copy.8 = bf16[16,6144]{1,0:T(8,128)(2,1)} copy(bf16[16,6144]{1,0:T(8,128)(2,1)} %shard_map.64) | data formatting | bytes 393216

commit v5 on v4

--- a/solution.py
+++ b/solution.py
@@ -395,14 +395,9 @@
     def _():
         arrive_last(1)
 
-    def end(pair, unused):
-        parts = (2 * pair, 2 * pair + 1)
-        attend(((jnp.where(full, last, z), 0), (last, jnp.where(full, 1, 0))), parts)
-        for part in parts:
-            finish(part)
-        return unused
-
-    lax.fori_loop(0, 2, end, 0)
+    attend(((jnp.where(full, last, z), 0), (last, jnp.where(full, 1, 0))), range(NX))
+    for part in range(NX):
+        finish(part)
 
     for at in range(EARLY, NZ):
         hand_on(jnp.int32(at))

time: 88 us -> 88.3 us (level)
  no operation moved by 1% of the time
where the time goes in v5:
time: 88.3 us; the launch traced here: 86.7 us
  Pallas kernels  85 us (96%)
  local copies, waits for them, and re-layouts  1.62 us (2%)
    pallas_call x1, Pallas kernels, local(): pl.pallas_call(kernel, out_shape=jax.ShapeDtypeStruct((MINE, D), bf16), i...  85 us

profile of v5, /device:TPU:6, one launch (start us, length us, event | category | flops | bytes accessed | tf_op | source)
XLA Modules:
  0.0 86.7 jit_solution(2604641073633520803)
XLA Ops:
  0.0 85.0 %shard_map.64 = bf16[16,6144]{1,0:T(8,128)(2,1)} custom-call(bf16[256,384]{1,0:T(8,128)(2,1)} %q_hbm.1, bf16[256,384]{1,0:T(8,128)(2,1)} %k_hbm.1, bf16[256,384]{1,0:T(8,128)(2,1)} %v_hbm.1, bf16[192,384]{1,0:T(8,128)(2,1)} %bitcast.3, s32[1,128]{1,0:T(1,128)} %bitcast.4, s32[1,128]{1,0:T(1,128)} %bitcast.5), custom_call_target="tpu_custom_call" | custom-call | flops 9797894144 | bytes 2097152 | tf_op jit(solution)/shard_map/pallas_call | solution.py:564
  85.0 1.6 %copy.8 = bf16[16,6144]{1,0:T(8,128)(2,1)} copy(bf16[16,6144]{1,0:T(8,128)(2,1)} %shard_map.64) | data formatting | bytes 393216
